TPU v7x, 32 devices: a whole 2x2x4 slice. The times are simulated.
32 devices in a mesh: grp: 2 (over y), fsdp: 8 (over z, x), seq: 2 (over core).
Axes of the slice: x: 2, y: 2, z: 4, core: 2. Of those that a mesh axis runs over, the one named last changes fastest.
Arguments:
- image_tokens: bfloat16 [16, 512, 3072], P(('grp', 'fsdp'), 'seq'), parts along dimension 0, may hold values from -6 to 6
- adjoint: bfloat16 [16, 512, 3072], P(('grp', 'fsdp'), 'seq'), parts along dimension 0, may hold values from -24 to 24
- attn_keys: bfloat16 [16, 768, 1536], P(('grp', 'fsdp'), 'seq'), parts along dimension 0, may hold values from -2.5 to 2.5
- attn_values: bfloat16 [16, 768, 1536], P(('grp', 'fsdp'), 'seq'), parts along dimension 0, may hold values from -6 to 6
- w_query: bfloat16 [3072, 1536], P('fsdp', 'seq'), may hold values from -0.109375 to 0.109375
- w_out: bfloat16 [1536, 3072], P('seq', 'fsdp'), may hold values from -0.15625 to 0.15625
- q_gain: float32 [128], replicated, may hold values from 1 to 2.5
- mod_table: float32 [28, 3, 3072], replicated, may hold values from -4 to 4
- timesteps: int32 [16], P(('grp', 'fsdp')), parts along dimension 0, may hold values from 0 to 27
- text_counts: int32 [16], P(('grp', 'fsdp')), parts along dimension 0, may hold values from 1 to 256
Outputs:
- branch_cotangent: float32 [16, 512, 3072], P(('grp', 'fsdp'), 'seq'), parts along dimension 0
There are 2 independent parts, one for each index of `grp`. A program takes and returns all parts, laid end to end along the dimension named above; an argument that names none is the same for every part. Nothing has to cross between parts.
Inputs may be any that keep to these rules, and one draw needn't show every extreme that they name: Of a prompt's 256 text keys, the first text_counts of them are real and the rest are padding.
All inputs are finite; a program needn't handle non-finite values.
Results may differ from a plain program's by a relative error of at most 0.0092.
Values may be sent and summed in bfloat16 or wider, within the bound.
A program may use at most 128 MiB of HBM per device.

v0:
```python
import jax
import jax.numpy as jnp
from jax import lax
from jax.sharding import PartitionSpec as P

HD = 128
SWAP = ((0, 1), (1, 0))


def contract_last(left, right):
    return lax.dot_general(
        left, right, (((1,), (1,)), ((), ())), preferred_element_type=jnp.float32
    )


def swap(piece):
    return lax.ppermute(piece, "seq", SWAP)


def local(
    image_tokens,
    adjoint,
    attn_keys,
    attn_values,
    w_query,
    w_out,
    q_gain,
    mod_table,
    timesteps,
    text_counts,
):
    me = lax.axis_index("seq")
    half = w_query.shape[1]
    heads = half // HD
    factor = HD ** (-0.5)
    w_q = lax.all_gather(w_query, "fsdp", axis=0, tiled=True)
    w_o = lax.all_gather(w_out.T, "fsdp", axis=0, tiled=True)
    modulation = lax.dynamic_index_in_dim(mod_table, timesteps[0], 0, keepdims=False)
    shift_row, scale_row, gate_row = (modulation[0], modulation[1], modulation[2])
    tokens = image_tokens[0].astype(jnp.float32)
    mean = jnp.mean(tokens, axis=-1, keepdims=True)
    centred = tokens - mean
    inv = lax.rsqrt(jnp.mean(centred * centred, axis=-1, keepdims=True) + 1e-06)
    normed = (centred * inv * (1.0 + scale_row) + shift_row).astype(jnp.bfloat16)
    d_branch = (gate_row * adjoint[0].astype(jnp.float32)).astype(jnp.bfloat16)

    def halves(rows):
        own = lax.dynamic_slice_in_dim(rows, me * half, half, 1)
        other = lax.dynamic_slice_in_dim(rows, (1 - me) * half, half, 1)
        return jnp.concatenate([own, swap(other)], axis=0)

    keys, values = (halves(attn_keys[0]), halves(attn_values[0]))
    key_rows = attn_keys.shape[1]
    txt = keys.shape[0] // 3
    spots = jnp.arange(key_rows, dtype=jnp.int32)
    positions = jnp.concatenate([me * key_rows + spots, (1 - me) * key_rows + spots])
    usable = (positions >= txt) | (positions < text_counts[0])
    normed_all = jnp.concatenate([normed, swap(normed)], axis=0)
    d_branch_all = jnp.concatenate([d_branch, swap(d_branch)], axis=0)
    query = jnp.dot(normed_all, w_q, preferred_element_type=jnp.float32)
    d_attn = jnp.dot(d_branch_all, w_o, preferred_element_type=jnp.float32).astype(jnp.bfloat16)
    parts = []
    for head in range(heads):
        cols = slice(head * HD, (head + 1) * HD)
        q_head, k_head, v_head = (query[:, cols], keys[:, cols], values[:, cols])
        root = lax.rsqrt(jnp.mean(q_head * q_head, axis=-1, keepdims=True) + 1e-06)
        unit = q_head * root
        q_normed = (unit * q_gain).astype(jnp.bfloat16)
        scores = contract_last(q_normed, k_head) * factor
        terms = jnp.where(usable[None, :], jnp.exp(scores), 0.0)
        probs = terms / jnp.sum(terms, axis=-1, keepdims=True)
        d_probs = contract_last(d_attn[:, cols], v_head)
        centre = jnp.sum(probs * d_probs, axis=-1, keepdims=True)
        d_scores = (probs * (d_probs - centre) * factor).astype(jnp.bfloat16)
        d_unit = jnp.dot(d_scores, k_head, preferred_element_type=jnp.float32) * q_gain
        d_query = root * (d_unit - unit * jnp.mean(d_unit * unit, axis=-1, keepdims=True))
        parts.append(d_query.astype(jnp.bfloat16))
    d_query = jnp.concatenate(parts, axis=1)
    count = tokens.shape[0]
    theirs = contract_last(d_query[count:], w_q).astype(jnp.bfloat16)
    mine = contract_last(d_query[:count], w_q)
    d_normed = mine + swap(theirs).astype(jnp.float32)
    d_hat = d_normed * (1.0 + scale_row)
    hat = centred * inv
    d_mean = jnp.mean(d_hat, axis=-1, keepdims=True)
    d_proj = jnp.mean(d_hat * hat, axis=-1, keepdims=True)
    return (inv * (d_hat - d_mean - hat * d_proj))[None]


def solution(mesh):
    in_specs = (
        P(("grp", "fsdp"), "seq", None),
        P(("grp", "fsdp"), "seq", None),
        P(("grp", "fsdp"), "seq", None),
        P(("grp", "fsdp"), "seq", None),
        P("fsdp", "seq"),
        P("seq", "fsdp"),
        P(),
        P(),
        P(("grp", "fsdp")),
        P(("grp", "fsdp")),
    )
    out_specs = P(("grp", "fsdp"), "seq", None)
    return jax.shard_map(local, mesh=mesh, in_specs=in_specs, out_specs=out_specs, check_vma=False)
```

profile of v0, /device:TPU:0, one launch (start us, length us, event | category | flops | bytes accessed | tf_op | source)
XLA Modules:
  0.0 214.6 jit_solution(10942834821170242803)
XLA Ops:
  6.5 0.7 all-gather.3.cloned.1.call-update
  7.3 0.0 all-gather.5.cloned.1.call-start
  7.3 0.7 all-gather.5.cloned.1.call-update
  8.7 1.7 convert_reduce_fusion
  10.4 0.6 fusion.12
  11.0 1.0 constant_dynamic-slice_fusion
  12.0 0.0 copy-start.9
  12.0 1.9 fusion.7
  13.9 0.5 collective-permute-start
  14.4 0.9 dynamic-slice_bitcast_fusion.2
  15.3 0.1 collective-permute-start.1
  15.3 0.5 copy-done.10
  15.9 0.9 dynamic-slice_bitcast_fusion
  16.8 0.1 collective-permute-start.3
  16.8 1.5 fusion.21
  18.3 0.5 collective-permute-start.2
  19.4 0.0 collective-permute-done.1
  19.5 0.0 collective-permute-done
  19.5 72.7 %all-gather.3.cloned.1.call-done = bf16[3072,768]{1,0:T(8,128)(2,1)} async-done(((bf16[384,768]{1,0:T(8,128)(2,1)}), bf16[3072,768]{1,0:T(8,128)(2,1)}) %all-gather.3.cloned.1.call-update) | async-done | bytes 4718608 | tf_op jit(solution)/shard_map/all_gather | solution.py:36
  92.2 5.9 %fusion.13 = f32[512,768]{1,0:T(8,128)S(1)} fusion(bf16[3072,768]{1,0:T(8,128)(2,1)} %all-gather.3.cloned.1.call-done, bf16[256,3072]{1,0:T(8,128)(2,1)} %collective-permute-done, bf16[256,3072]{1,0:T(8,128)(2,1)} %fusion.7), kind=kOutput, calls=%fused_computation.16 | convolution fusion | flops 2422210560 | bytes 9437184 | tf_op jit(solution)/shard_map/dot_general | solution.py:60
  98.1 0.0 copy-start.23
  98.1 0.5 multiply_reduce_fusion.7
  98.6 0.1 copy-done.23
  98.7 2.2 %fusion.116 = (f32[512]{0:T(512)}, f32[512,768]{1,0:T(8,128)}) fusion(bf16[384,768]{1,0:T(8,128)(2,1)S(1)} %get-tuple-element.20, bf16[384,768]{1,0:T(8,128)(2,1)S(1)} %collective-permute-done.1, f32[512,768]{1,0:T(8,128)S(1)} %fusion.13, f32[512]{0:T(512)S(1)} %get-tuple-element.56, f32[128]{0:T(128)S(1)} %copy-done.23, pred[768]{0:T(1024)(128)(4,1)S(1)} %compare_or_fusion), kind=kOutput, calls=%fused_computation.213 | convolution fusion | flops 102432256 | bytes 3020288 | tf_op jit(solution)/shard_map/dot_general | solution.py:11
  101.0 2.2 %fusion.111 = (f32[512]{0:T(512)}, f32[512,768]{1,0:T(8,128)}) fusion(bf16[384,768]{1,0:T(8,128)(2,1)S(1)} %get-tuple-element.20, bf16[384,768]{1,0:T(8,128)(2,1)S(1)} %collective-permute-done.1, f32[512,768]{1,0:T(8,128)S(1)} %fusion.13, f32[128]{0:T(128)S(1)} %copy-done.23, f32[512]{0:T(512)S(1)} %get-tuple-element.57, pred[768]{0:T(1024)(128)(4,1)S(1)} %compare_or_fusion), kind=kOutput, calls=%fused_computation.208 | convolution fusion | flops 102432256 | bytes 3020288 | tf_op jit(solution)/shard_map/dot_general | solution.py:11
  103.2 2.3 %fusion.114 = (f32[512]{0:T(512)}, f32[512,768]{1,0:T(8,128)}) fusion(bf16[384,768]{1,0:T(8,128)(2,1)S(1)} %get-tuple-element.20, bf16[384,768]{1,0:T(8,128)(2,1)S(1)} %collective-permute-done.1, f32[512,768]{1,0:T(8,128)S(1)} %fusion.13, f32[512]{0:T(512)S(1)} %get-tuple-element.54, f32[128]{0:T(128)S(1)} %copy-done.23, pred[768]{0:T(1024)(128)(4,1)S(1)} %compare_or_fusion), kind=kOutput, calls=%fused_computation.211 | convolution fusion | flops 102432256 | bytes 3020288 | tf_op jit(solution)/shard_map/dot_general | solution.py:11
  105.5 2.2 %fusion.115 = (f32[512]{0:T(512)}, f32[512,768]{1,0:T(8,128)}) fusion(bf16[384,768]{1,0:T(8,128)(2,1)S(1)} %get-tuple-element.20, bf16[384,768]{1,0:T(8,128)(2,1)S(1)} %collective-permute-done.1, f32[512,768]{1,0:T(8,128)S(1)} %fusion.13, f32[512]{0:T(512)S(1)} %get-tuple-element.55, f32[128]{0:T(128)S(1)} %copy-done.23, pred[768]{0:T(1024)(128)(4,1)S(1)} %compare_or_fusion), kind=kOutput, calls=%fused_computation.212 | convolution fusion | flops 102432256 | bytes 3020288 | tf_op jit(solution)/shard_map/dot_general | solution.py:11
  107.7 2.2 %fusion.113 = (f32[512]{0:T(512)}, f32[512,768]{1,0:T(8,128)}) fusion(bf16[384,768]{1,0:T(8,128)(2,1)S(1)} %get-tuple-element.20, bf16[384,768]{1,0:T(8,128)(2,1)S(1)} %collective-permute-done.1, f32[512,768]{1,0:T(8,128)S(1)} %fusion.13, f32[512]{0:T(512)S(1)} %get-tuple-element.53, f32[128]{0:T(128)S(1)} %copy-done.23, pred[768]{0:T(1024)(128)(4,1)S(1)} %compare_or_fusion), kind=kOutput, calls=%fused_computation.210 | convolution fusion | flops 102432256 | bytes 3020288 | tf_op jit(solution)/shard_map/dot_general | solution.py:11
  109.9 2.2 %fusion.112 = (f32[512]{0:T(512)}, f32[512,768]{1,0:T(8,128)}) fusion(bf16[768,128]{1,0:T(8,128)(2,1)S(1)} %pad_maximum_fusion.2, f32[512,768]{1,0:T(8,128)S(1)} %fusion.13, f32[512]{0:T(512)S(1)} %get-tuple-element.52, f32[128]{0:T(128)S(1)} %copy-done.23, pred[768]{0:T(1024)(128)(4,1)S(1)} %compare_or_fusion), kind=kOutput, calls=%fused_computation.209 | convolution fusion | flops 102039040 | bytes 2037248 | tf_op jit(solution)/shard_map/dot_general | solution.py:11
  112.1 0.0 collective-permute-done.2
  112.1 61.2 %all-gather.5.cloned.1.call-done = bf16[3072,768]{0,1:T(8,128)(2,1)} async-done(((bf16[384,768]{0,1:T(8,128)(2,1)}), bf16[3072,768]{0,1:T(8,128)(2,1)}) %all-gather.5.cloned.1.call-update) | async-done | bytes 4718608 | tf_op jit(solution)/shard_map/all_gather | solution.py:37
  173.4 6.0 %fusion.22 = bf16[512,768]{1,0:T(8,128)(2,1)S(1)} fusion(bf16[3072,768]{0,1:T(8,128)(2,1)} %all-gather.5.cloned.1.call-done, bf16[256,3072]{1,0:T(8,128)(2,1)} %collective-permute-done.2, bf16[256,3072]{1,0:T(8,128)(2,1)} %fusion.21), kind=kOutput, calls=%fused_computation.65 | convolution fusion | flops 2422603776 | bytes 8650752 | tf_op jit(solution)/shard_map/dot_general | solution.py:61
  179.4 0.0 collective-permute-done.3
  179.5 0.0 copy-start.24
  179.5 1.4 multiply_reduce_fusion.4
  180.9 0.0 copy-start.8
  180.9 0.5 convolution_multiply_fusion.4
  181.4 0.9 copy-done.8
  182.3 1.4 multiply_reduce_fusion.5
  183.7 0.5 convolution_multiply_fusion.5
  184.2 0.9 copy-done.6
  185.1 1.4 multiply_reduce_fusion.2
  186.5 0.7 convolution_multiply_fusion.2
  187.1 0.7 copy-done.5
  187.9 1.4 multiply_reduce_fusion.3
  189.2 0.5 convolution_multiply_fusion.3
  189.7 0.9 copy-done.4
  190.6 1.5 multiply_reduce_fusion.1
  192.1 1.4 multiply_reduce_fusion
  193.6 0.5 convolution_multiply_fusion.1
  194.1 0.8 copy-done.2
  195.0 0.0 slice-start.1
  195.0 1.2 multiply_reduce_fusion.6
  196.2 0.2 fusion.63
  196.4 0.3 fusion.64
  196.7 0.3 fusion.65
  196.9 0.3 fusion.66
  197.2 0.3 fusion.67
  197.4 0.3 fusion.68
  197.8 1.4 convolution_convert_fusion
  199.2 0.1 collective-permute-start.4
  199.3 3.4 %collective-permute-done.4 = bf16[256,3072]{1,0:T(8,128)(2,1)S(1)} collective-permute-done((bf16[256,3072]{1,0:T(8,128)(2,1)S(1)}, bf16[256,3072]{1,0:T(8,128)(2,1)S(1)}, u32[]{:S(2)}, u32[]{:S(2)}) %collective-permute-start.4) | collective-permute-done | bytes 1572896 | tf_op jit(solution)/shard_map/ppermute | solution.py:17
  202.7 2.0 fusion.25
  204.7 3.0 %fusion.11 = f32[1,256,3072]{2,1,0:T(8,128)} fusion(bf16[1,256,3072]{2,1,0:T(8,128)(2,1)S(1)} %copy-done, f32[256]{0:T(256)S(1)} %broadcast_multiply_fusion.6, f32[256]{0:T(256)S(1)} %broadcast_multiply_fusion.7, f32[256]{0:T(256)S(1)} %copy-done.26, f32[256]{0:T(256)S(1)} %copy-done.22, f32[3072]{0:T(1024)S(1)} %bitcast.60, ...), kind=kLoop, calls=%fused_computation.14 | loop fusion | flops 7864320 | bytes 9453568 | tf_op jit(solution)/shard_map/broadcast_in_dim | solution.py:87
  (82 shorter events, 0.2 us)
Async XLA Ops:
  6.5 3.8 %copy-start = (bf16[1,256,3072]{2,1,0:T(8,128)(2,1)S(1)}, bf16[1,256,3072]{2,1,0:T(8,128)(2,1)}, u32[]{:S(2)}) copy-start(bf16[1,256,3072]{2,1,0:T(8,128)(2,1)} %param.10) | copy-start | bytes 4718596
  6.5 85.6 %all-gather.3.cloned.1.call-start = ((), (), s32[]{:S(2)}) async-start(), calls=%async_computation | async-start | bytes 5308416 | tf_op jit(solution)/shard_map/all_gather | solution.py:36
  7.3 166.1 %all-gather.5.cloned.1.call-start = ((), (), s32[]{:S(2)}) async-start(), calls=%async_computation.1 | async-start | bytes 5308416 | tf_op jit(solution)/shard_map/all_gather | solution.py:37
  10.4 3.6 %copy-start.21 = (f32[256]{0:T(256)}, f32[256]{0:T(256)S(1)}, u32[]{:S(2)}) copy-start(f32[256]{0:T(256)S(1)} %broadcast_multiply_fusion.8) | copy-start | bytes 3076
  10.9 3.0 %copy-start.25 = (f32[256]{0:T(256)}, f32[256]{0:T(256)S(1)}, u32[]{:S(2)}) copy-start(f32[256]{0:T(256)S(1)} %add_rsqrt_fusion.6) | copy-start | bytes 3076
  12.0 2.4 %copy-start.9 = (bf16[1,384,1536]{2,1,0:T(8,128)(2,1)S(1)}, bf16[1,384,1536]{2,1,0:T(8,128)(2,1)}, u32[]{:S(2)}) copy-start(bf16[1,384,1536]{2,1,0:T(8,128)(2,1)} %param.12) | copy-start | bytes 3538948
  13.9 5.5 %collective-permute-start = (bf16[256,3072]{1,0:T(8,128)(2,1)}, bf16[256,3072]{1,0:T(8,128)(2,1)}, u32[]{:S(2)}, u32[]{:S(2)}) collective-permute-start(bf16[256,3072]{1,0:T(8,128)(2,1)} %fusion.7), channel_id=1, source_target_pairs={{0,1},{1,0},{2,3},{3,2},{4,5},{5,4},{6,7},{7,6},{8,9},{9,8},{10,11... | collective-permute-start | bytes 4718600 | tf_op jit(solution)/shard_map/ppermute | solution.py:17
  14.4 1.5 copy-start.10
  15.3 1.6 copy-start.3
  15.3 4.2 %collective-permute-start.1 = (bf16[384,768]{1,0:T(8,128)(2,1)}, bf16[384,768]{1,0:T(8,128)(2,1)S(1)}, u32[]{:S(2)}, u32[]{:S(2)}) collective-permute-start(bf16[384,768]{1,0:T(8,128)(2,1)} %get-tuple-element.19), channel_id=1, source_target_pairs={{0,1},{1,0},{2,3},{3,2},{4,5},{5,4},{6,7},{7,6},{8,9},{9,8},{10,11... | collective-permute-start | bytes 1769480 | tf_op jit(solution)/shard_map/ppermute | solution.py:17
  16.8 162.7 %collective-permute-start.3 = (bf16[384,768]{1,0:T(8,128)(2,1)}, bf16[384,768]{1,0:T(8,128)(2,1)}, u32[]{:S(2)}, u32[]{:S(2)}) collective-permute-start(bf16[384,768]{1,0:T(8,128)(2,1)} %get-tuple-element.24), channel_id=1, source_target_pairs={{0,1},{1,0},{2,3},{3,2},{4,5},{5,4},{6,7},{7,6},{8,9},{9,8},{10,11... | collective-permute-start | bytes 1769480 | tf_op jit(solution)/shard_map/ppermute | solution.py:17
  18.3 93.9 %collective-permute-start.2 = (bf16[256,3072]{1,0:T(8,128)(2,1)}, bf16[256,3072]{1,0:T(8,128)(2,1)}, u32[]{:S(2)}, u32[]{:S(2)}) collective-permute-start(bf16[256,3072]{1,0:T(8,128)(2,1)} %fusion.21), channel_id=1, source_target_pairs={{0,1},{1,0},{2,3},{3,2},{4,5},{5,4},{6,7},{7,6},{8,9},{9,8},{10,11... | collective-permute-start | bytes 4718600 | tf_op jit(solution)/shard_map/ppermute | solution.py:17
  98.1 11.8 %copy-start.1 = (f32[512,768]{1,0:T(8,128)}, f32[512,768]{1,0:T(8,128)S(1)}, u32[]{:S(2)}) copy-start(f32[512,768]{1,0:T(8,128)S(1)} %fusion.13) | copy-start | bytes 4718596
  98.1 0.7 copy-start.23
  98.6 9.1 %copy-start.11 = (f32[512]{0:T(512)}, f32[512]{0:T(512)S(1)}, u32[]{:S(2)}) copy-start(f32[512]{0:T(512)S(1)} %get-tuple-element.53) | copy-start | bytes 6148
  98.6 11.3 %copy-start.27 = (f32[512]{0:T(512)}, f32[512]{0:T(512)S(1)}, u32[]{:S(2)}) copy-start(f32[512]{0:T(512)S(1)} %get-tuple-element.52) | copy-start | bytes 6148
  98.6 2.3 %copy-start.15 = (f32[512]{0:T(512)}, f32[512]{0:T(512)S(1)}, u32[]{:S(2)}) copy-start(f32[512]{0:T(512)S(1)} %get-tuple-element.56) | copy-start | bytes 6148
  98.6 4.6 %copy-start.17 = (f32[512]{0:T(512)}, f32[512]{0:T(512)S(1)}, u32[]{:S(2)}) copy-start(f32[512]{0:T(512)S(1)} %get-tuple-element.57) | copy-start | bytes 6148
  101.0 4.5 %copy-start.13 = (f32[512]{0:T(512)}, f32[512]{0:T(512)S(1)}, u32[]{:S(2)}) copy-start(f32[512]{0:T(512)S(1)} %get-tuple-element.54) | copy-start | bytes 6148
  101.0 4.5 %copy-start.19 = (f32[512]{0:T(512)}, f32[512]{0:T(512)S(1)}, u32[]{:S(2)}) copy-start(f32[512]{0:T(512)S(1)} %get-tuple-element.55) | copy-start | bytes 6148
  112.1 67.3 %copy-start.32 = (f32[512]{0:T(512)S(1)}, f32[512]{0:T(512)}, u32[]{:S(2)}) copy-start(f32[512]{0:T(512)} %get-tuple-element.46) | copy-start | bytes 6148
  173.4 6.1 %copy-start.7 = (f32[512,768]{1,0:T(8,128)S(1)}, f32[512,768]{1,0:T(8,128)}, u32[]{:S(2)}) copy-start(f32[512,768]{1,0:T(8,128)} %get-tuple-element.47) | copy-start | bytes 4718596
  179.5 1.4 copy-start.24
  180.9 1.4 copy-start.8
  180.9 1.4 copy-start.33
  183.7 1.4 copy-start.6
  183.7 1.4 copy-start.31
  186.4 1.4 copy-start.5
  186.4 1.4 copy-start.30
  189.2 1.4 copy-start.4
  189.2 1.4 copy-start.29
  190.6 1.5 copy-start.34
  190.6 1.5 copy-start.35
  193.5 1.4 copy-start.2
  193.5 1.4 copy-start.12
  193.5 1.4 copy-start.14
  193.5 1.4 copy-start.16
  193.5 1.4 copy-start.18
  193.6 1.4 copy-start.20
  193.6 1.4 copy-start.28
  193.6 4.1 %slice-start = ((s8[4718592]{0:T(1024)(128)(4,1)}), s8[4194304]{0:T(1024)(128)(4,1)S(1)}, s32[]{:S(2)}) async-start(s8[4718592]{0:T(1024)(128)(4,1)} %bitcast.63), calls=%async_computation.2 | async-start | bytes 8388608
  195.0 2.8 %slice-start.1 = ((s8[4718592]{0:T(1024)(128)(4,1)}), s8[524288]{0:T(1024)(128)(4,1)S(1)}, s32[]{:S(2)}) async-start(s8[4718592]{0:T(1024)(128)(4,1)} %bitcast.63), calls=%async_computation.3 | async-start | bytes 1048576
  197.7 4.9 %copy-start.22 = (f32[256]{0:T(256)S(1)}, f32[256]{0:T(256)}, u32[]{:S(2)}) copy-start(f32[256]{0:T(256)} %copy-done.21) | copy-start | bytes 3076
  197.7 4.9 %copy-start.26 = (f32[256]{0:T(256)S(1)}, f32[256]{0:T(256)}, u32[]{:S(2)}) copy-start(f32[256]{0:T(256)} %copy-done.25) | copy-start | bytes 3076
  199.2 3.5 %collective-permute-start.4 = (bf16[256,3072]{1,0:T(8,128)(2,1)S(1)}, bf16[256,3072]{1,0:T(8,128)(2,1)S(1)}, u32[]{:S(2)}, u32[]{:S(2)}) collective-permute-start(bf16[256,3072]{1,0:T(8,128)(2,1)S(1)} %convolution_convert_fusion), channel_id=1, source_target_pairs={{0,1},{1,0},{2,3},{3,2},{4,5},{5,4},{6,7},{7,6},{8,9},{9,8},{10,11... | collective-permute-start | bytes 4718600 | tf_op jit(solution)/shard_map/ppermute | solution.py:17
Sparse Core Ops, SparseCore 0:
  9.5 82.5 all-gather.2
  94.2 79.1 all-gather.4
where the time goes:
time: 215 us
  waiting for transfers between devices  139 us (65%)
  matrix products  40.9 us (19%)
  between operations  15.3 us (7%)
  other arithmetic  11.8 us (5%)
  local copies, waits for them, and re-layouts  6.78 us (3%)
    all_gather x1, waiting for transfers between devices, local(): w_q = lax.all_gather(w_query, 'fsdp', axis=0, tiled=True)  72.7 us
    all_gather x1, waiting for transfers between devices, local(): w_o = lax.all_gather(w_out.T, 'fsdp', axis=0, tiled=True)  61.2 us
    dot_general x14, matrix products, contract_last(): lax.dot_general(left, right, (((1,), (1,)), ((), ())), preferred_element_...  25.1 us
    dot_general x1, matrix products, local(): jnp.dot(d_branch_all, w_o, preferred_element_type=jnp.float32)  6.04 us
    dot_general x1, matrix products, local(): query = jnp.dot(normed_all, w_q, preferred_element_type=jnp.float32)  5.89 us
    unnamed x76, local copies, waits for them, and re-layouts  5.01 us
  transfers between devices with their start and end apart: 7, of which 3 were waited for; matrix products, arithmetic and copies ran while one was open for 16% of the time, Pallas kernels for 0%

commit v1 on v0

--- a/solution.py
+++ b/solution.py
@@ -29,11 +29,27 @@
     timesteps,
     text_counts,
 ):
+
+    def try_all_marks(local_block, comm_axis):
+        workers = jax.lax.axis_size(comm_axis)
+        all_blocks = []
+        for d in range(workers):
+            all_blocks.append((d, (d + 1) % workers))
+        arr_now = [None] * workers
+        arr_now[workers - 1] = local_block
+        for dev_i in range(workers - 2, -1, -1):
+            arr_now[dev_i] = jax.lax.ppermute(arr_now[dev_i + 1], comm_axis, all_blocks)
+        return jnp.roll(
+            jnp.concatenate(arr_now, 0),
+            (jax.lax.axis_index(comm_axis) + 1) * local_block.shape[0],
+            0,
+        )
+
     me = lax.axis_index("seq")
     half = w_query.shape[1]
     heads = half // HD
     factor = HD ** (-0.5)
-    w_q = lax.all_gather(w_query, "fsdp", axis=0, tiled=True)
+    w_q = try_all_marks(w_query, "fsdp")
     w_o = lax.all_gather(w_out.T, "fsdp", axis=0, tiled=True)
     modulation = lax.dynamic_index_in_dim(mod_table, timesteps[0], 0, keepdims=False)
     shift_row, scale_row, gate_row = (modulation[0], modulation[1], modulation[2])

time: 215 us -> 230 us (1.070)
  local copies, waits for them, and re-layouts: 6.78 us -> 19.3 us
  starting transfers between devices: 1.13 us -> 3.52 us
    ppermute x0 -> x7, waiting for transfers between devices: none -> 135 us  [try_all_marks(): arr_now[dev_i] = jax.lax.ppermute(arr_now[dev_i + 1], comm_axis, all_blocks)]
    all_gather x1 -> x0, waiting for transfers between devices: 72.7 us -> none  [local(): w_q = lax.all_gather(w_query, 'fsdp', axis=0, tiled=True)]
    all_gather x1, waiting for transfers between devices: 61.2 us -> 0.01 us  [local(): w_o = lax.all_gather(w_out.T, 'fsdp', axis=0, tiled=True)]
    unnamed x76 -> x97, local copies, waits for them, and re-layouts: 5.01 us -> 16 us
    ppermute x0 -> x7, starting transfers between devices: none -> 2.95 us  [try_all_marks(): arr_now[dev_i] = jax.lax.ppermute(arr_now[dev_i + 1], comm_axis, all_blocks)]
  transfers between devices with their start and end apart: 7 -> 13, of which waited for: 3 -> 8; matrix products, arithmetic and copies ran while one was open for 16% -> 20% of each run, Pallas kernels for 0% -> 0%
where the time goes in v1:
time: 230 us; the launch traced here: 229 us
  waiting for transfers between devices  138 us (60%)
  matrix products  42.3 us (18%)
  local copies, waits for them, and re-layouts  19.3 us (8%)
  between operations  15.4 us (7%)
  other arithmetic  10.1 us (4%)
  starting transfers between devices  3.52 us (2%)
    ppermute x7, waiting for transfers between devices, try_all_marks(): arr_now[dev_i] = jax.lax.ppermute(arr_now[dev_i + 1], comm_axis, all_blocks)  135 us
    dot_general x14, matrix products, contract_last(): lax.dot_general(left, right, (((1,), (1,)), ((), ())), preferred_element_...  25.6 us
    unnamed x97, local copies, waits for them, and re-layouts  16 us
    dot_general x1, matrix products, local(): query = jnp.dot(normed_all, w_q, preferred_element_type=jnp.float32)  6.94 us
    dot_general x1, matrix products, local(): jnp.dot(d_branch_all, w_o, preferred_element_type=jnp.float32)  6.07 us
  transfers between devices with their start and end apart: 13, of which 8 were waited for; matrix products, arithmetic and copies ran while one was open for 20% of the time, Pallas kernels for 0%

profile of v1, /device:TPU:0, one launch (start us, length us, event | category | flops | bytes accessed | tf_op | source)
XLA Modules:
  0.0 228.9 jit_solution(4010455965681873788)
XLA Ops:
  6.5 2.9 %collective-permute-start.1 = (bf16[384,768]{1,0:T(8,128)(2,1)}, bf16[384,768]{1,0:T(8,128)(2,1)S(1)}, u32[]{:S(2)}, u32[]{:S(2)}) collective-permute-start(bf16[384,768]{1,0:T(8,128)(2,1)} %param.14), channel_id=1, source_target_pairs={{0,2},{2,4},{4,6},{6,8},{8,10},{10,12},{12,14},{14,0},{1,3},{3,5},... | collective-permute-start | bytes 1769480 | tf_op jit(solution)/shard_map/ppermute | solution.py:41
  9.5 16.6 %collective-permute-done.1 = bf16[384,768]{1,0:T(8,128)(2,1)S(1)} collective-permute-done((bf16[384,768]{1,0:T(8,128)(2,1)}, bf16[384,768]{1,0:T(8,128)(2,1)S(1)}, u32[]{:S(2)}, u32[]{:S(2)}) %collective-permute-start.1) | collective-permute-done | bytes 589856 | tf_op jit(solution)/shard_map/ppermute | solution.py:41
  26.1 17.2 %collective-permute-done.2 = bf16[384,768]{1,0:T(8,128)(2,1)S(1)} collective-permute-done((bf16[384,768]{1,0:T(8,128)(2,1)S(1)}, bf16[384,768]{1,0:T(8,128)(2,1)S(1)}, u32[]{:S(2)}, u32[]{:S(2)}) %collective-permute-start.2) | collective-permute-done | bytes 589856 | tf_op jit(solution)/shard_map/ppermute | solution.py:41
  43.3 16.4 %collective-permute-done.3 = bf16[384,768]{1,0:T(8,128)(2,1)} collective-permute-done((bf16[384,768]{1,0:T(8,128)(2,1)S(1)}, bf16[384,768]{1,0:T(8,128)(2,1)}, u32[]{:S(2)}, u32[]{:S(2)}) %collective-permute-start.3) | collective-permute-done | bytes 589856 | tf_op jit(solution)/shard_map/ppermute | solution.py:41
  59.7 2.1 dynamic-slice_bitcast_fusion.2
  61.8 0.3 convert_reduce_fusion
  62.2 14.2 %collective-permute-done.4 = bf16[384,768]{1,0:T(8,128)(2,1)} collective-permute-done((bf16[384,768]{1,0:T(8,128)(2,1)}, bf16[384,768]{1,0:T(8,128)(2,1)}, u32[]{:S(2)}, u32[]{:S(2)}) %collective-permute-start.4) | collective-permute-done | bytes 589856 | tf_op jit(solution)/shard_map/ppermute | solution.py:41
  76.4 0.6 fusion.17
  77.6 1.0 dynamic-slice_add_fusion
  78.7 24.4 %collective-permute-done.5 = bf16[384,768]{1,0:T(8,128)(2,1)} collective-permute-done((bf16[384,768]{1,0:T(8,128)(2,1)}, bf16[384,768]{1,0:T(8,128)(2,1)}, u32[]{:S(2)}, u32[]{:S(2)}) %collective-permute-start.5) | collective-permute-done | bytes 589856 | tf_op jit(solution)/shard_map/ppermute | solution.py:41
  103.1 1.9 fusion.12
  105.0 1.1 dynamic-slice_bitcast_fusion
  106.2 0.5 collective-permute-start.10
  106.6 19.4 %collective-permute-done.6 = bf16[384,768]{1,0:T(8,128)(2,1)} collective-permute-done((bf16[384,768]{1,0:T(8,128)(2,1)}, bf16[384,768]{1,0:T(8,128)(2,1)}, u32[]{:S(2)}, u32[]{:S(2)}) %collective-permute-start.6) | collective-permute-done | bytes 589856 | tf_op jit(solution)/shard_map/ppermute | solution.py:41
  126.0 1.5 fusion.25
  128.2 26.6 %collective-permute-done.7 = bf16[384,768]{1,0:T(8,128)(2,1)} collective-permute-done((bf16[384,768]{1,0:T(8,128)(2,1)}, bf16[384,768]{1,0:T(8,128)(2,1)}, u32[]{:S(2)}, u32[]{:S(2)}) %collective-permute-start.7) | collective-permute-done | bytes 589856 | tf_op jit(solution)/shard_map/ppermute | solution.py:41
  154.8 1.1 constant_dynamic-update-slice_fusion.15
  155.9 1.1 constant_dynamic-update-slice_fusion.14
  157.1 1.2 constant_dynamic-update-slice_fusion.13
  158.2 1.1 constant_dynamic-update-slice_fusion.12
  159.4 1.2 constant_dynamic-update-slice_fusion.11
  160.7 1.1 constant_dynamic-update-slice_fusion.7
  161.8 1.1 constant_dynamic-update-slice_fusion.6
  162.9 1.1 constant_dynamic-update-slice_fusion.5
  164.0 1.1 constant_dynamic-update-slice_fusion.4
  165.1 1.1 constant_dynamic-update-slice_fusion.3
  166.4 6.9 %fusion.3 = f32[512,768]{1,0:T(8,128)S(1)} fusion(bf16[6144,768]{1,0:T(8,128)(2,1)S(1)} %constant_dynamic-update-slice_fusion, s32[]{:T(128)S(6)} %select_n.46, bf16[256,3072]{1,0:T(8,128)(2,1)} %collective-permute-done, bf16[256,3072]{1,0:T(8,128)(2,1)} %fusion.12), kind=kOutput, calls=%fused_computation.7 | convolution fusion | flops 2422210560 | bytes 9437188 | tf_op jit(solution)/shard_map/dot_general | solution.py:76
  173.4 0.5 multiply_reduce_fusion.7
  173.9 0.1 copy-done.25
  174.1 2.2 fusion.117
  176.3 2.2 fusion.119
  178.5 2.2 fusion.120
  180.7 2.2 fusion.121
  182.9 2.2 fusion.122
  185.1 2.3 fusion.118
  187.4 6.1 %fusion.26 = bf16[512,768]{1,0:T(8,128)(2,1)S(1)} fusion(bf16[3072,768]{0,1:T(8,128)(2,1)} %all-gather.2.cloned.1.call-done, bf16[256,3072]{1,0:T(8,128)(2,1)} %collective-permute-done.9, bf16[256,3072]{1,0:T(8,128)(2,1)} %fusion.25), kind=kOutput, calls=%fused_computation.69 | convolution fusion | flops 2422603776 | bytes 8650752 | tf_op jit(solution)/shard_map/dot_general | solution.py:77
  193.5 1.4 multiply_reduce_fusion.5
  194.9 0.5 convolution_multiply_fusion.5
  195.5 0.9 copy-done.10
  196.3 1.4 multiply_reduce_fusion.1
  197.7 0.5 convolution_multiply_fusion.1
  198.2 0.9 copy-done.9
  199.1 1.4 multiply_reduce_fusion.2
  200.5 0.5 convolution_multiply_fusion.2
  200.9 0.9 copy-done.8
  201.9 1.4 multiply_reduce_fusion.3
  203.2 0.7 convolution_multiply_fusion.3
  203.9 0.7 copy-done.7
  204.6 1.4 multiply_reduce_fusion.4
  206.1 0.5 convolution_multiply_fusion.4
  206.5 0.9 copy-done.36
  207.4 1.5 multiply_reduce_fusion
  209.0 1.1 multiply_reduce_fusion.6
  210.1 0.2 fusion.65
  210.4 0.3 fusion.66
  210.7 0.3 fusion.67
  210.9 0.3 fusion.68
  211.2 0.3 fusion.69
  211.5 0.3 fusion.70
  211.8 1.4 convolution_convert_fusion
  213.3 0.1 collective-permute-start.11
  213.3 3.4 %collective-permute-done.11 = bf16[256,3072]{1,0:T(8,128)(2,1)S(1)} collective-permute-done((bf16[256,3072]{1,0:T(8,128)(2,1)S(1)}, bf16[256,3072]{1,0:T(8,128)(2,1)S(1)}, u32[]{:S(2)}, u32[]{:S(2)}) %collective-permute-start.11) | collective-permute-done | bytes 1572896 | tf_op jit(solution)/shard_map/ppermute | solution.py:17
  216.7 2.5 %fusion.116 = (f32[256]{0:T(256)S(1)}, f32[256]{0:T(256)S(1)}, f32[256,3072]{1,0:T(8,128)S(1)}) fusion(f32[256]{0:T(256)S(1)} %copy-done.28, f32[256]{0:T(256)S(1)} %copy-done.24, bf16[1,256,3072]{2,1,0:T(8,128)(2,1)S(1)} %copy-done, f32[3072]{0:T(1024)S(1)} %bitcast.56, bf16[256,3072]{1,0:T(8,128)(2,1)S(1)} %collective-permute-done.11, ...), kind=kOutput, calls=%fused_computation.229 | convolution fusion | flops 1215036928 | bytes 11419652 | tf_op jit(solution)/shard_map/dot_general | solution.py:11
  219.3 2.8 %fusion.16 = f32[1,256,3072]{2,1,0:T(8,128)} fusion(bf16[1,256,3072]{2,1,0:T(8,128)(2,1)S(1)} %copy-done, f32[256,3072]{1,0:T(8,128)S(1)} %get-tuple-element.51, f32[256]{0:T(256)S(1)} %broadcast_multiply_fusion.6, f32[256]{0:T(256)S(1)} %broadcast_multiply_fusion.7, f32[256]{0:T(256)S(1)} %copy-done.28, f32[256]{0:T(256)S(1)} %copy-done.24), kind=kLoop, calls=%fused_computation.20 | loop fusion | flops 5505024 | bytes 7868416 | tf_op jit(solution)/shard_map/broadcast_in_dim | solution.py:103
  (115 shorter events, 0.6 us)
Async XLA Ops:
  6.5 55.3 %copy-start = (bf16[1,256,3072]{2,1,0:T(8,128)(2,1)S(1)}, bf16[1,256,3072]{2,1,0:T(8,128)(2,1)}, u32[]{:S(2)}) copy-start(bf16[1,256,3072]{2,1,0:T(8,128)(2,1)} %param.10) | copy-start | bytes 4718596
  6.5 180.8 %all-gather.2.cloned.1.call-start = ((), (), s32[]{:S(2)}) async-start(), calls=%async_computation | async-start | bytes 5308416 | tf_op jit(solution)/shard_map/all_gather | solution.py:53
  6.5 19.5 %collective-permute-start.1 = (bf16[384,768]{1,0:T(8,128)(2,1)}, bf16[384,768]{1,0:T(8,128)(2,1)S(1)}, u32[]{:S(2)}, u32[]{:S(2)}) collective-permute-start(bf16[384,768]{1,0:T(8,128)(2,1)} %param.14), channel_id=1, source_target_pairs={{0,2},{2,4},{4,6},{6,8},{8,10},{10,12},{12,14},{14,0},{1,3},{3,5},... | collective-permute-start | bytes 1769480 | tf_op jit(solution)/shard_map/ppermute | solution.py:41
  26.1 17.2 %collective-permute-start.2 = (bf16[384,768]{1,0:T(8,128)(2,1)S(1)}, bf16[384,768]{1,0:T(8,128)(2,1)S(1)}, u32[]{:S(2)}, u32[]{:S(2)}) collective-permute-start(bf16[384,768]{1,0:T(8,128)(2,1)S(1)} %collective-permute-done.1), channel_id=1, source_target_pairs={{0,2},{2,4},{4,6},{6,8},{8,10},{10,12},{12,14},{14,0},{1,3},{3,5},... | collective-permute-start | bytes 1769480 | tf_op jit(solution)/shard_map/ppermute | solution.py:41
  43.3 18.6 %copy-start.4 = (bf16[384,768]{1,0:T(8,128)(2,1)}, bf16[384,768]{1,0:T(8,128)(2,1)S(1)}, u32[]{:S(2)}) copy-start(bf16[384,768]{1,0:T(8,128)(2,1)S(1)} %collective-permute-done.2) | copy-start | bytes 1769476
  43.3 16.4 %collective-permute-start.3 = (bf16[384,768]{1,0:T(8,128)(2,1)S(1)}, bf16[384,768]{1,0:T(8,128)(2,1)}, u32[]{:S(2)}, u32[]{:S(2)}) collective-permute-start(bf16[384,768]{1,0:T(8,128)(2,1)S(1)} %collective-permute-done.2), channel_id=1, source_target_pairs={{0,2},{2,4},{4,6},{6,8},{8,10},{10,12},{12,14},{14,0},{1,3},{3,5},... | collective-permute-start | bytes 1769480 | tf_op jit(solution)/shard_map/ppermute | solution.py:41
  59.7 16.7 %collective-permute-start.4 = (bf16[384,768]{1,0:T(8,128)(2,1)}, bf16[384,768]{1,0:T(8,128)(2,1)}, u32[]{:S(2)}, u32[]{:S(2)}) collective-permute-start(bf16[384,768]{1,0:T(8,128)(2,1)} %collective-permute-done.3), channel_id=1, source_target_pairs={{0,2},{2,4},{4,6},{6,8},{8,10},{10,12},{12,14},{14,0},{1,3},{3,5},... | collective-permute-start | bytes 1769480 | tf_op jit(solution)/shard_map/ppermute | solution.py:41
  61.8 66.3 %collective-permute-start.8 = (bf16[384,768]{1,0:T(8,128)(2,1)}, bf16[384,768]{1,0:T(8,128)(2,1)S(1)}, u32[]{:S(2)}, u32[]{:S(2)}) collective-permute-start(bf16[384,768]{1,0:T(8,128)(2,1)} %get-tuple-element.19), channel_id=1, source_target_pairs={{0,1},{1,0},{2,3},{3,2},{4,5},{5,4},{6,7},{7,6},{8,9},{9,8},{10,11... | collective-permute-start | bytes 1769480 | tf_op jit(solution)/shard_map/ppermute | solution.py:17
  62.1 42.9 %copy-start.23 = (f32[256]{0:T(256)}, f32[256]{0:T(256)S(1)}, u32[]{:S(2)}) copy-start(f32[256]{0:T(256)S(1)} %broadcast_multiply_fusion.8) | copy-start | bytes 3076
  76.4 26.7 %collective-permute-start.5 = (bf16[384,768]{1,0:T(8,128)(2,1)}, bf16[384,768]{1,0:T(8,128)(2,1)}, u32[]{:S(2)}, u32[]{:S(2)}) collective-permute-start(bf16[384,768]{1,0:T(8,128)(2,1)} %collective-permute-done.4), channel_id=1, source_target_pairs={{0,2},{2,4},{4,6},{6,8},{8,10},{10,12},{12,14},{14,0},{1,3},{3,5},... | collective-permute-start | bytes 1769480 | tf_op jit(solution)/shard_map/ppermute | solution.py:41
  77.6 27.4 %copy-start.27 = (f32[256]{0:T(256)}, f32[256]{0:T(256)S(1)}, u32[]{:S(2)}) copy-start(f32[256]{0:T(256)S(1)} %add_rsqrt_fusion.6) | copy-start | bytes 3076
  103.1 22.9 %collective-permute-start.6 = (bf16[384,768]{1,0:T(8,128)(2,1)}, bf16[384,768]{1,0:T(8,128)(2,1)}, u32[]{:S(2)}, u32[]{:S(2)}) collective-permute-start(bf16[384,768]{1,0:T(8,128)(2,1)} %collective-permute-done.5), channel_id=1, source_target_pairs={{0,2},{2,4},{4,6},{6,8},{8,10},{10,12},{12,14},{14,0},{1,3},{3,5},... | collective-permute-start | bytes 1769480 | tf_op jit(solution)/shard_map/ppermute | solution.py:41
  103.1 1.9 copy-start.12
  105.0 21.0 %copy-start.6 = (bf16[1,256,3072]{2,1,0:T(8,128)(2,1)S(1)}, bf16[1,256,3072]{2,1,0:T(8,128)(2,1)}, u32[]{:S(2)}) copy-start(bf16[1,256,3072]{2,1,0:T(8,128)(2,1)} %param.11) | copy-start | bytes 4718596
  105.0 61.4 %collective-permute-start = (bf16[256,3072]{1,0:T(8,128)(2,1)}, bf16[256,3072]{1,0:T(8,128)(2,1)}, u32[]{:S(2)}, u32[]{:S(2)}) collective-permute-start(bf16[256,3072]{1,0:T(8,128)(2,1)} %fusion.12), channel_id=1, source_target_pairs={{0,1},{1,0},{2,3},{3,2},{4,5},{5,4},{6,7},{7,6},{8,9},{9,8},{10,11... | collective-permute-start | bytes 4718600 | tf_op jit(solution)/shard_map/ppermute | solution.py:17
  106.2 87.3 %collective-permute-start.10 = (bf16[384,768]{1,0:T(8,128)(2,1)}, bf16[384,768]{1,0:T(8,128)(2,1)}, u32[]{:S(2)}, u32[]{:S(2)}) collective-permute-start(bf16[384,768]{1,0:T(8,128)(2,1)} %get-tuple-element.24), channel_id=1, source_target_pairs={{0,1},{1,0},{2,3},{3,2},{4,5},{5,4},{6,7},{7,6},{8,9},{9,8},{10,11... | collective-permute-start | bytes 1769480 | tf_op jit(solution)/shard_map/ppermute | solution.py:17
  126.0 28.8 %collective-permute-start.7 = (bf16[384,768]{1,0:T(8,128)(2,1)}, bf16[384,768]{1,0:T(8,128)(2,1)}, u32[]{:S(2)}, u32[]{:S(2)}) collective-permute-start(bf16[384,768]{1,0:T(8,128)(2,1)} %collective-permute-done.6), channel_id=1, source_target_pairs={{0,2},{2,4},{4,6},{6,8},{8,10},{10,12},{12,14},{14,0},{1,3},{3,5},... | collective-permute-start | bytes 1769480 | tf_op jit(solution)/shard_map/ppermute | solution.py:41
  127.5 59.9 %collective-permute-start.9 = (bf16[256,3072]{1,0:T(8,128)(2,1)}, bf16[256,3072]{1,0:T(8,128)(2,1)}, u32[]{:S(2)}, u32[]{:S(2)}) collective-permute-start(bf16[256,3072]{1,0:T(8,128)(2,1)} %fusion.25), channel_id=1, source_target_pairs={{0,1},{1,0},{2,3},{3,2},{4,5},{5,4},{6,7},{7,6},{8,9},{9,8},{10,11... | collective-permute-start | bytes 4718600 | tf_op jit(solution)/shard_map/ppermute | solution.py:17
  157.0 3.5 %copy-start.5 = (bf16[384,768]{1,0:T(8,128)(2,1)S(1)}, bf16[384,768]{1,0:T(8,128)(2,1)}, u32[]{:S(2)}) copy-start(bf16[384,768]{1,0:T(8,128)(2,1)} %copy-done.4) | copy-start | bytes 1769476
  159.3 1.3 copy-start.3
  166.4 7.0 %copy-start.14 = (bf16[6144,768]{1,0:T(8,128)(2,1)}, bf16[6144,768]{1,0:T(8,128)(2,1)S(1)}, u32[]{:S(2)}) copy-start(bf16[6144,768]{1,0:T(8,128)(2,1)S(1)} %constant_dynamic-update-slice_fusion) | copy-start | bytes 28311556
  173.4 11.7 %copy-start.1 = (f32[512,768]{1,0:T(8,128)}, f32[512,768]{1,0:T(8,128)S(1)}, u32[]{:S(2)}) copy-start(f32[512,768]{1,0:T(8,128)S(1)} %fusion.3) | copy-start | bytes 4718596
  173.4 0.7 copy-start.25
  173.9 2.4 %copy-start.21 = (f32[512]{0:T(512)}, f32[512]{0:T(512)S(1)}, u32[]{:S(2)}) copy-start(f32[512]{0:T(512)S(1)} %get-tuple-element.57) | copy-start | bytes 6148
  173.9 9.0 %copy-start.15 = (f32[512]{0:T(512)}, f32[512]{0:T(512)S(1)}, u32[]{:S(2)}) copy-start(f32[512]{0:T(512)S(1)} %get-tuple-element.56) | copy-start | bytes 6148
  173.9 11.2 %copy-start.29 = (f32[512]{0:T(512)}, f32[512]{0:T(512)S(1)}, u32[]{:S(2)}) copy-start(f32[512]{0:T(512)S(1)} %get-tuple-element.52) | copy-start | bytes 6148
  176.3 4.4 %copy-start.17 = (f32[512]{0:T(512)}, f32[512]{0:T(512)S(1)}, u32[]{:S(2)}) copy-start(f32[512]{0:T(512)S(1)} %get-tuple-element.54) | copy-start | bytes 6148
  176.3 4.4 %copy-start.19 = (f32[512]{0:T(512)}, f32[512]{0:T(512)S(1)}, u32[]{:S(2)}) copy-start(f32[512]{0:T(512)S(1)} %get-tuple-element.55) | copy-start | bytes 6148
  187.4 6.1 %copy-start.13 = (bf16[384,768]{1,0:T(8,128)(2,1)S(1)}, bf16[384,768]{1,0:T(8,128)(2,1)}, u32[]{:S(2)}) copy-start(bf16[384,768]{1,0:T(8,128)(2,1)} %get-tuple-element.25) | copy-start | bytes 1769476
  187.4 6.1 %copy-start.11 = (f32[512,768]{1,0:T(8,128)S(1)}, f32[512,768]{1,0:T(8,128)}, u32[]{:S(2)}) copy-start(f32[512,768]{1,0:T(8,128)} %get-tuple-element.27) | copy-start | bytes 4718596
  193.5 1.4 copy-start.26
  193.5 1.4 copy-start.35
  194.9 1.4 copy-start.10
  194.9 1.4 copy-start.34
  197.7 1.4 copy-start.9
  197.7 1.4 copy-start.33
  200.4 1.4 copy-start.8
  200.5 1.4 copy-start.32
  203.2 1.4 copy-start.7
  203.2 1.4 copy-start.31
  206.0 1.4 copy-start.36
  206.0 1.4 copy-start.37
  206.0 2.9 %copy-start.16 = (f32[512]{0:T(512)S(1)}, f32[512]{0:T(512)}, u32[]{:S(2)}) copy-start(f32[512]{0:T(512)} %copy-done.15) | copy-start | bytes 6148
  206.0 2.9 %copy-start.18 = (f32[512]{0:T(512)S(1)}, f32[512]{0:T(512)}, u32[]{:S(2)}) copy-start(f32[512]{0:T(512)} %copy-done.17) | copy-start | bytes 6148
  206.0 2.9 %copy-start.20 = (f32[512]{0:T(512)S(1)}, f32[512]{0:T(512)}, u32[]{:S(2)}) copy-start(f32[512]{0:T(512)} %copy-done.19) | copy-start | bytes 6148
  206.0 2.9 %copy-start.22 = (f32[512]{0:T(512)S(1)}, f32[512]{0:T(512)}, u32[]{:S(2)}) copy-start(f32[512]{0:T(512)} %copy-done.21) | copy-start | bytes 6148
  206.0 2.9 %copy-start.30 = (f32[512]{0:T(512)S(1)}, f32[512]{0:T(512)}, u32[]{:S(2)}) copy-start(f32[512]{0:T(512)} %copy-done.29) | copy-start | bytes 6148
  207.4 1.6 copy-start.2
  207.4 4.3 %slice-start = ((s8[9437184]{0:T(1024)(128)(4,1)}), s8[4194304]{0:T(1024)(128)(4,1)S(1)}, s32[]{:S(2)}) async-start(s8[9437184]{0:T(1024)(128)(4,1)} %bitcast.59), calls=%async_computation.1 | async-start | bytes 8388608
  207.4 4.3 %slice-start.1 = ((s8[9437184]{0:T(1024)(128)(4,1)}), s8[4194304]{0:T(1024)(128)(4,1)S(1)}, s32[]{:S(2)}) async-start(s8[9437184]{0:T(1024)(128)(4,1)} %bitcast.59), calls=%async_computation.2 | async-start | bytes 8388608
  209.0 2.8 %slice-start.2 = ((s8[9437184]{0:T(1024)(128)(4,1)}), s8[1048576]{0:T(1024)(128)(4,1)S(1)}, s32[]{:S(2)}) async-start(s8[9437184]{0:T(1024)(128)(4,1)} %bitcast.59), calls=%async_computation.3 | async-start | bytes 2097152
  211.8 4.9 %copy-start.24 = (f32[256]{0:T(256)S(1)}, f32[256]{0:T(256)}, u32[]{:S(2)}) copy-start(f32[256]{0:T(256)} %copy-done.23) | copy-start | bytes 3076
  211.8 4.9 %copy-start.28 = (f32[256]{0:T(256)S(1)}, f32[256]{0:T(256)}, u32[]{:S(2)}) copy-start(f32[256]{0:T(256)} %copy-done.27) | copy-start | bytes 3076
  213.3 3.5 %collective-permute-start.11 = (bf16[256,3072]{1,0:T(8,128)(2,1)S(1)}, bf16[256,3072]{1,0:T(8,128)(2,1)S(1)}, u32[]{:S(2)}, u32[]{:S(2)}) collective-permute-start(bf16[256,3072]{1,0:T(8,128)(2,1)S(1)} %convolution_convert_fusion), channel_id=1, source_target_pairs={{0,1},{1,0},{2,3},{3,2},{4,5},{5,4},{6,7},{7,6},{8,9},{9,8},{10,11... | collective-permute-start | bytes 4718600 | tf_op jit(solution)/shard_map/ppermute | solution.py:17
Sparse Core Ops, SparseCore 0:
  59.8 111.3 all-gather.1
